TPU v7x, 512 devices: a whole 4x4x16 slice. The times are simulated.
512 devices in a mesh: dp: 16 (over x, y), tensor: 32 (over z, core).
Axes of the slice: x: 4, y: 4, z: 16, core: 2. Of those that a mesh axis runs over, the one named last changes fastest.
Arguments:
- query_rows: bfloat16 [2560, 4096], P('dp', 'tensor'), may hold values from -12 to 12
- key_rows: bfloat16 [2560, 4096], P('dp', 'tensor'), may hold values from -12 to 12
- value_rows: bfloat16 [2560, 4096], P('dp', 'tensor'), may hold values from -6 to 6
- out_weight: bfloat16 [4096, 5120], P('tensor'), may hold values from -0.09375 to 0.09375
- encoder: bfloat16 [40, 128, 32], replicated, may hold values from -0.5 to 0.5
- decoder: bfloat16 [40, 32, 128], replicated, may hold values from -1 to 1
- positions: int32 [2560], P('dp'), may hold values from 0 to 159, as said below
- cotangent: bfloat16 [2560, 5120], P(('dp', 'tensor')), may hold values from -1.796875 to 1.796875
Outputs:
- attended: bfloat16 [2560, 5120], P(('dp', 'tensor'))
- grad_query: bfloat16 [2560, 4096], P('dp', 'tensor')
- grad_key: bfloat16 [2560, 4096], P('dp', 'tensor')
- grad_value: bfloat16 [2560, 4096], P('dp', 'tensor')
- grad_weight: bfloat16 [4096, 5120], P('tensor')
Inputs may be any that keep to these rules, and one draw needn't show every extreme that they name: `positions`: within each sequence of 160 tokens, the first token has position 0 and every other token's position is 0 or its predecessor's plus one.
All inputs are finite; a program needn't handle non-finite values.
Results may differ from a plain program's by a relative error of at most 0.03.
Values may be sent and summed in bfloat16 or wider, within the bound.
A program may use at most 64 MiB of HBM per device.

v0:
```python
import jax
import jax.numpy as jnp
from jax import lax
from jax.sharding import PartitionSpec as P

HEAD = 128
LEN = 160


def encode(partial_value, encoder):
    row_count = partial_value.shape[0]
    blocks, width, narrow = encoder.shape
    shaped = partial_value.reshape(row_count, blocks, width)
    result = jnp.einsum(
        "rbi,bio->rbo", shaped, encoder.astype(jnp.float32), precision=lax.Precision.HIGHEST
    )
    return result.reshape(row_count, blocks * narrow)


def decode(code_rows, decoder):
    row_count = code_rows.shape[0]
    blocks, narrow, width = decoder.shape
    shaped = code_rows.reshape(row_count, blocks, narrow)
    result = jnp.einsum(
        "rbo,boi->rbi", shaped, decoder.astype(jnp.float32), precision=lax.Precision.HIGHEST
    )
    return result.reshape(row_count, blocks * width)


def compress(grad_rows, decoder):
    row_count = grad_rows.shape[0]
    blocks, narrow, width = decoder.shape
    shaped = grad_rows.reshape(row_count, blocks, width)
    result = jnp.einsum(
        "rbi,boi->rbo", shaped, decoder.astype(jnp.float32), precision=lax.Precision.HIGHEST
    )
    return result.reshape(row_count, blocks * narrow)


def expand(code_rows, encoder):
    row_count = code_rows.shape[0]
    blocks, width, narrow = encoder.shape
    shaped = code_rows.reshape(row_count, blocks, narrow)
    result = jnp.einsum(
        "rbo,bio->rbi", shaped, encoder.astype(jnp.float32), precision=lax.Precision.HIGHEST
    )
    return result.reshape(row_count, blocks * width)


def attend(queries, key_vals, values, doc_pos):
    seq_len = queries.shape[1]
    score_scale = queries.shape[3] ** (-0.5)
    scores = (
        jnp.einsum("sqhd,skhd->shqk", queries, key_vals, preferred_element_type=jnp.float32)
        * score_scale
    )
    place = jnp.arange(seq_len, dtype=jnp.int32)
    visible = (place[None, None, :] <= place[None, :, None]) & (
        place[None, None, :] >= place[None, :, None] - doc_pos[:, :, None]
    )
    scores = jnp.where(visible[:, None], scores, jnp.float32(-1e30))
    largest = jnp.max(scores, axis=-1, keepdims=True)
    exps = jnp.exp(scores - largest)
    attn_prob = exps / jnp.sum(exps, axis=-1, keepdims=True)
    attn_bf = attn_prob.astype(jnp.bfloat16)
    context = jnp.einsum(
        "shqk,skhd->sqhd", attn_bf, values, preferred_element_type=jnp.float32
    ).astype(jnp.bfloat16)
    return (attn_prob, attn_bf, context)


def attend_back(queries, key_vals, values, attn_prob, attn_bf, grad_context):
    score_scale = queries.shape[3] ** (-0.5)
    grad_value = jnp.einsum(
        "shqk,sqhd->skhd", attn_bf, grad_context, preferred_element_type=jnp.float32
    ).astype(jnp.bfloat16)
    grad_prob = jnp.einsum(
        "sqhd,skhd->shqk", grad_context, values, preferred_element_type=jnp.float32
    )
    row_dot = jnp.sum(attn_prob * grad_prob, axis=-1, keepdims=True)
    grad_score = (attn_prob * (grad_prob - row_dot) * score_scale).astype(jnp.bfloat16)
    grad_query = jnp.einsum(
        "shqk,skhd->sqhd", grad_score, key_vals, preferred_element_type=jnp.float32
    ).astype(jnp.bfloat16)
    grad_key = jnp.einsum(
        "shqk,sqhd->skhd", grad_score, queries, preferred_element_type=jnp.float32
    ).astype(jnp.bfloat16)
    return (grad_query, grad_key, grad_value)


def local(query_rows, key_rows, value_rows, out_weight, encoder, decoder, positions, cotangent):
    group_rows = query_rows.shape[0]
    width = query_rows.shape[1]
    seq_count = group_rows // LEN
    shape4 = (seq_count, LEN, width // HEAD, HEAD)
    queries = query_rows.reshape(shape4)
    key_vals = key_rows.reshape(shape4)
    values = value_rows.reshape(shape4)
    attn_prob, attn_bf, context4 = attend(
        queries, key_vals, values, positions.reshape(seq_count, LEN)
    )
    context = context4.reshape(group_rows, width)
    context_rows = context
    partial_value = jnp.dot(context_rows, out_weight, preferred_element_type=jnp.float32)
    code_sum = lax.psum_scatter(
        encode(partial_value, encoder).astype(jnp.bfloat16),
        "tensor",
        scatter_dimension=0,
        tiled=True,
    ).astype(jnp.float32)
    attended = decode(code_sum, decoder).astype(jnp.bfloat16)
    grad_code = compress(cotangent.astype(jnp.float32), decoder).astype(jnp.bfloat16)
    expanded_rows = expand(
        lax.all_gather(grad_code, "tensor", axis=0, tiled=True).astype(jnp.float32), encoder
    )
    context_rows = context
    upper_part = expanded_rows.astype(jnp.bfloat16)
    lower_part = (expanded_rows - upper_part.astype(jnp.float32)).astype(jnp.bfloat16)
    weight_acc = jnp.dot(context_rows.T, upper_part, preferred_element_type=jnp.float32)
    weight_acc = weight_acc + jnp.dot(
        context_rows.T, lower_part, preferred_element_type=jnp.float32
    )
    local_grad = jnp.dot(upper_part, out_weight.T, preferred_element_type=jnp.float32)
    context_acc = local_grad
    weight_acc, context_acc = (weight_acc, context_acc)
    grad_weight = lax.psum(weight_acc.astype(jnp.bfloat16), "dp")
    grad_context = context_acc.astype(jnp.bfloat16).reshape(shape4)
    grad_query, grad_key, grad_value = attend_back(
        queries, key_vals, values, attn_prob, attn_bf, grad_context
    )
    return (
        attended,
        grad_query.reshape(group_rows, width),
        grad_key.reshape(group_rows, width),
        grad_value.reshape(group_rows, width),
        grad_weight,
    )


def solution(mesh):
    placed = (
        P("dp", "tensor"),
        P("dp", "tensor"),
        P("dp", "tensor"),
        P("tensor", None),
        P(),
        P(),
        P("dp"),
        P(("dp", "tensor"), None),
    )
    return jax.shard_map(
        local,
        mesh=mesh,
        in_specs=placed,
        out_specs=(
            P(("dp", "tensor"), None),
            P("dp", "tensor"),
            P("dp", "tensor"),
            P("dp", "tensor"),
            P("tensor", None),
        ),
        check_vma=False,
    )
```

profile of v0, /device:TPU:1, one launch (start us, length us, event | category | flops | bytes accessed | tf_op | source)
XLA Modules:
  0.0 350.1 jit_solution(6105032515843861662)
XLA Ops:
  7.2 0.0 all-reduce.6.cloned.1.call-start
  7.3 1.8 copy.29
  9.1 0.2 fusion.32
  9.3 0.1 fusion.23
  9.4 0.2 convolution_convert_fusion.6
  9.6 0.6 fusion.26
  10.2 3.2 convolution_convert_fusion
  13.5 1.0 copy.22
  14.5 0.0 all-reduce.6.cloned.1.call-update
  14.5 0.0 all-reduce.4.cloned.1.call-start
  14.5 0.3 fusion.15
  14.8 0.1 reshape.148
  15.0 39.4 %all-gather = bf16[32,5,1280]{2,1,0:T(8,128)(2,1)S(1)} all-gather(bf16[1,5,1280]{2,1,0:T(8,128)(2,1)S(1)} %reshape.148), channel_id=1, replica_groups=mesh['dp'=16,'tensor'=32] {'tensor'}, dimensions={0}, use_global_device_ids=true | all-gather | bytes 422400 | tf_op jit(solution)/shard_map/all_gather | solution.py:114
  54.3 1.3 reshape.144
  55.7 0.6 fusion.9
  56.2 0.5 fusion.5
  56.8 1.1 copy-done.1
  57.9 1.6 fusion
  59.5 1.3 copy-done.2
  60.8 2.5 fusion.16
  63.3 0.2 multiply_reduce_fusion
  63.5 1.3 dynamic-slice
  65.5 0.1 multiply_convert_fusion
  65.5 0.8 convolution_convert_fusion.5
  66.3 0.8 convolution_convert_fusion.4
  67.1 0.8 fusion.19
  67.9 153.2 %all-reduce.6.cloned.1.call-done = bf16[160,1280]{1,0:T(8,128)(2,1)} async-done(((bf16[160,1280]{1,0:T(8,128)(2,1)}), bf16[160,1280]{1,0:T(8,128)(2,1)}) %all-reduce.6.cloned.1.call-update) | async-done | bytes 409616
  221.1 0.8 constant_dynamic-slice_fusion
  221.9 0.1 reshape.142
  222.0 0.8 fusion.14
  222.8 117.9 %all-reduce.4.cloned.1.call-done = bf16[128,5120]{1,0:T(8,128)(2,1)} async-done(((bf16[128,5120]{1,0:T(8,128)(2,1)}), bf16[128,5120]{1,0:T(8,128)(2,1)}) %all-reduce.4.cloned.1.call-update) | async-done | bytes 1310736 | tf_op jit(solution)/shard_map/psum | solution.py:126
  340.8 2.5 copy.52
  (19 shorter events, 0.1 us)
Async XLA Ops:
  7.2 3.0 copy-start
  7.2 1.9 copy-start.7
  7.2 1.9 copy-start.6
  7.2 1.9 copy-start.5
  7.2 2.2 copy-start.8
  7.2 213.9 %all-reduce.6.cloned.1.call-start = ((), (), s32[]{:S(2)}) async-start(), calls=%async_computation.1 | async-start | bytes 819200
  10.2 4.3 %copy-start.3 = (bf16[40,32,128]{2,1,0:T(8,128)(2,1)S(1)}, bf16[40,32,128]{2,1,0:T(8,128)(2,1)}, u32[]{:S(2)}) copy-start(bf16[40,32,128]{2,1,0:T(8,128)(2,1)} %param.13) | copy-start | bytes 983044
  10.2 4.3 %copy-start.4 = (bf16[5,5120]{1,0:T(8,128)(2,1)S(1)}, bf16[5,5120]{1,0:T(8,128)(2,1)}, u32[]{:S(2)}) copy-start(bf16[5,5120]{1,0:T(8,128)(2,1)} %param.15) | copy-start | bytes 153604
  14.5 326.3 %all-reduce.4.cloned.1.call-start = ((), (), s32[]{:S(2)}) async-start(), calls=%async_computation | async-start | bytes 2621440 | tf_op jit(solution)/shard_map/psum | solution.py:126
  56.2 1.7 copy-start.1
  59.5 1.3 copy-start.2
Sparse Core Ops, SparseCore 0:
  14.6 206.4 all-reduce.5
  225.3 115.4 all-reduce.3
where the time goes:
time: 351 us; the launch traced here: 350 us
  waiting for transfers between devices  271 us (77%)
  blocking collectives  39.4 us (11%)
  between operations  14.9 us (4%)
  matrix products  13.2 us (4%)
  local copies, waits for them, and re-layouts  11.3 us (3%)
    unnamed x3, waiting for transfers between devices  153 us
    psum x1, waiting for transfers between devices, local(): grad_weight = lax.psum(weight_acc.astype(jnp.bfloat16), 'dp')  118 us
    all_gather x1, blocking collectives, local(): lax.all_gather(grad_code, 'tensor', axis=0, tiled=True).astype(jnp.float32)  39.4 us
    unnamed x22, local copies, waits for them, and re-layouts  7.09 us
  transfers between devices with their start and end apart: 2, of which 2 were waited for; matrix products, arithmetic and copies ran while one was open for 4% of the time, Pallas kernels for 0%

commit v1 on v0

v1 whole, which is shorter than its diff:
```python
import functools

import jax
import jax.numpy as jnp
from jax import lax
from jax.experimental import pallas as pl
from jax.experimental.pallas import tpu as pltpu
from jax.sharding import PartitionSpec as P

MESH = pl.DeviceIdType.MESH
F32 = jnp.float32
BF16 = jnp.bfloat16

LEN = 160
HEAD = 128
WIDTH = 5120
CODE = 1280
TILES = CODE // 128
OWN = 5
PAD = 8
SLOTS = 32
MSG = 64
DP = 16
NT = (((1,), (1,)), ((), ()))
TN = (((0,), (0,)), ((), ()))


def dot(a, b, dims=(((1,), (0,)), ((), ()))):
    return lax.dot_general(a, b, dims, preferred_element_type=F32)


def lane_groups(rows):
    return lax.broadcasted_iota(jnp.int32, (rows, 128), 1) // 32


def core_kernel(
    q_hbm, k_hbm, v_hbm, w_hbm, enc_hbm, dec_hbm, pos_hbm, cot_hbm,
    sum_out, att_out, gq_out, gk_out, gv_out, enc,
    q, k, v, w, dec, pos, cot, cot8, gst, gbuf, ust, gpad, perm, attn, ctx, ctx_t, spread, wenc,
    pst, psnd, psib, pone, prec1, ptwo, prec2, code, mpart, mrecv, mfull,
    in_sem, send_sem, recv_sem,
):
    dp = lax.axis_index("dp")
    t = lax.axis_index("tensor")
    core = lax.rem(t, 2)
    sign = 1 - 2 * core

    def chip(dz):
        return {"tensor": lax.rem(t + 2 * dz + SLOTS, SLOTS)}

    sibling = {"tensor": t + sign}

    def plane(d):
        return {"dp": lax.rem(dp + d, DP)}

    loads = []
    for n, (src, dst) in enumerate(
        ((cot_hbm, cot), (dec_hbm, dec), (q_hbm, q), (k_hbm, k), (v_hbm, v), (pos_hbm, pos), (enc_hbm, enc), (w_hbm, w))
    ):
        c = pltpu.make_async_copy(src, dst, in_sem.at[n])
        c.start()
        loads.append(c)
    cot_in, dec_in, q_in, k_in, v_in, pos_in, enc_in, w_in = loads

    barrier = pltpu.get_barrier_semaphore()
    partners = [sibling] + [chip(dz) for dz in (8, 4, -4, 2, -2, 1, -1)] + [plane(d) for d in range(1, DP)]
    for device in partners:
        pl.semaphore_signal(barrier, inc=1, device_id=device, device_id_type=MESH)

    count = [0]
    started = []

    def send(src, dst, device):
        n = count[0]
        count[0] = n + 1
        c = pltpu.make_async_remote_copy(
            src_ref=src, dst_ref=dst, send_sem=send_sem.at[n], recv_sem=recv_sem.at[n],
            device_id=device, device_id_type=MESH,
        )
        c.start()
        started.append(c)
        return c

    cot8[...] = jnp.zeros_like(cot8)
    gst[...] = jnp.zeros_like(gst)
    groups8 = lane_groups(PAD)
    cot_in.wait()
    dec_in.wait()
    cot8[0:OWN, :] = cot[...].astype(F32)
    for j in range(TILES):
        rows = jnp.concatenate([cot8[:, 512 * j + 128 * i : 512 * j + 128 * (i + 1)] for i in range(4)], axis=0)
        full = dot(rows.astype(BF16), dec[4 * j : 4 * j + 4].reshape(128, 128), NT)
        tile = jnp.zeros((PAD, 128), F32)
        for i in range(4):
            tile = tile + jnp.where(groups8 == i, full[PAD * i : PAD * (i + 1)], 0.0)
        gst[OWN * j : OWN * j + PAD, :] = tile
    gbuf[0, 0, 0] = gst[...].astype(BF16)

    pl.semaphore_wait(barrier, len(partners))

    steps = (0, 1, 2 * sign, -1)
    g_far = [None] + [send(gbuf.at[0, 0, 0], gbuf.at[0, 0, 4 - n], chip(4 * n)) for n in (2, 1, 3)]
    g_near = [None] + [send(gbuf.at[0, 0, 0], gbuf.at[0, p, 0], chip(-steps[p])) for p in (1, 2, 3)]

    row = lax.broadcasted_iota(jnp.int32, (SLOTS * PAD, LEN), 0)
    col = lax.broadcasted_iota(jnp.int32, (SLOTS * PAD, LEN), 1)
    slot = row // PAD
    other = slot // 16
    near = (slot // 4) % 4
    far = slot % 4
    step = jnp.where(near == 1, 1, jnp.where(near == 2, 2 * sign * (1 - 2 * other), jnp.where(near == 3, -1, 0)))
    at_chip = (t // 2 + step + 4 * far + 16) % 16
    token = OWN * (2 * at_chip + (core + other) % 2) + row % PAD
    valid = row % PAD < OWN
    perm[...] = jnp.where(valid & (token == col), 1.0, 0.0).astype(BF16)

    q_in.wait()
    k_in.wait()
    v_in.wait()
    pos_in.wait()
    scale = HEAD ** (-0.5)
    qp = dot(perm[...], q[...]).astype(BF16)
    pos8 = jnp.broadcast_to(pos[...].reshape(1, LEN), (PAD, LEN)).astype(F32).astype(BF16)
    pos_col = dot(perm[...], pos8, NT)[:, 0:1].astype(jnp.int32)
    scores = dot(qp, k[...], NT) * scale
    visible = (col <= token) & (col >= token - pos_col)
    scores = jnp.where(visible, scores, F32(-1e30))
    exps = jnp.exp(scores - jnp.max(scores, axis=-1, keepdims=True))
    probs = exps / jnp.sum(exps, axis=-1, keepdims=True)
    attn[...] = probs
    ctx_f = dot(probs.astype(BF16), v[...])
    ctx[...] = ctx_f.astype(BF16)
    ctx_t[...] = ctx_f.T.astype(BF16)

    enc_in.wait()
    code_group = lax.broadcasted_iota(jnp.int32, (128, 128), 0) // 32
    for j in range(TILES):
        group = enc[4 * j : 4 * j + 4].reshape(128, 128)
        for i in range(4):
            spread[j, :, 128 * i : 128 * (i + 1)] = jnp.where(code_group == i, group, jnp.zeros_like(group))

    w_in.wait()
    for j in range(TILES):
        part = dot(w[:, 512 * j : 512 * (j + 1)], spread[j], NT).astype(BF16)
        wenc[:, 128 * j : 128 * (j + 1)] = part
        pst[:, OWN * j : OWN * j + PAD, :] = dot(ctx[...], part).reshape(SLOTS, PAD, 128)
    pst[:, MSG - 8 : MSG, :] = jnp.zeros((SLOTS, 8, 128), F32)
    psnd[...] = pst[16:32].reshape(4, 4, MSG, 128).astype(BF16)
    p_sib = send(psnd, psib, sibling)

    for c in g_far[1:]:
        c.wait_recv()
    g_pack = [None] + [send(gbuf.at[0, 0, pl.ds(1, 3)], gbuf.at[0, p, pl.ds(1, 3)], chip(-steps[p])) for p in (1, 2, 3)]
    g_over = [send(gbuf.at[0, 0], gbuf.at[1, 0], sibling)]

    p_sib.wait_recv()
    for p in range(4):
        pst[4 * p : 4 * p + 4] = pst[4 * p : 4 * p + 4] + psib[p].astype(F32)
        if p:
            pone[p] = pst[4 * p : 4 * p + 4].astype(BF16)
    p_near = [None] + [send(pone.at[p], prec1.at[p], chip(steps[p])) for p in (1, 2, 3)]

    def unpack(other_core):
        for p in range(4):
            ust[4 * p : 4 * p + 4] = gbuf[other_core, p].astype(F32)
        keep = lax.broadcasted_iota(jnp.int32, (16, PAD, 128), 1) < OWN
        for j in range(TILES):
            block = jnp.where(keep, ust[:, OWN * j : OWN * j + PAD, :], 0.0)
            gpad[128 * other_core : 128 * (other_core + 1), 128 * j : 128 * (j + 1)] = block.reshape(128, 128).astype(BF16)

    for p in (1, 3, 2):
        g_near[p].wait_recv()
        g_pack[p].wait_recv()
        g_over.append(send(gbuf.at[0, p], gbuf.at[1, p], sibling))
    unpack(0)
    for c in g_over:
        c.wait_recv()
    unpack(1)

    for half in range(2):
        part = dot(ctx_t[...], gpad[:, 640 * half : 640 * (half + 1)]).astype(BF16)
        for r in range(8):
            mpart[2 * r + half] = part[16 * r : 16 * (r + 1)]
    m_parts = []
    for d in range(1, DP):
        m_parts.append(send(mpart.at[lax.rem(dp + d, DP)], mrecv.at[d], plane(d)))

    for c in p_near[1:]:
        c.wait_recv()
    for n in range(4):
        total = pst[n]
        for p in (1, 2, 3):
            total = total + prec1[p, n].astype(F32)
        if n:
            ptwo[n] = total.astype(BF16)
        else:
            code[0:MSG] = total
    p_far = [None] + [send(ptwo.at[n], prec2.at[n], chip(4 * n)) for n in (2, 1, 3)]

    gc = dot(gpad[...], wenc[...], NT).astype(BF16)
    probs = attn[...]
    gv_out[...] = dot(probs.astype(BF16), gc, TN).astype(BF16)
    g_prob = dot(gc, v[...], NT)
    row_dot = jnp.sum(probs * g_prob, axis=-1, keepdims=True)
    g_score = (probs * (g_prob - row_dot) * scale).astype(BF16)
    gq_out[...] = dot(perm[...], dot(g_score, k[...]).astype(BF16), TN).astype(BF16)
    gk_out[...] = dot(g_score, qp, TN).astype(BF16)

    for c in m_parts:
        c.wait_recv()
    total = mpart[dp].astype(F32)
    for d in range(1, DP):
        total = total + mrecv[d].astype(F32)
    mfull[dp] = total.astype(BF16)
    m_sums = [send(mfull.at[dp], mfull.at[dp], plane(d)) for d in range(1, DP)]

    for c in p_far[1:]:
        c.wait_recv()
    total = code[0:MSG]
    for n in (1, 2, 3):
        total = total + prec2[n].astype(F32)
    code[0:MSG] = total
    for j in range(TILES):
        rows = code[OWN * j : OWN * j + PAD, :]
        rows = jnp.concatenate([jnp.where(groups8 == i, rows, 0.0) for i in range(4)], axis=0)
        full = dot(rows.astype(BF16), dec[4 * j : 4 * j + 4].reshape(128, 128))
        for i in range(4):
            att_out[:, 512 * j + 128 * i : 512 * j + 128 * (i + 1)] = full[PAD * i : PAD * i + OWN].astype(BF16)

    for c in m_sums:
        c.wait_recv()
    sum_out[...] = mfull[...]
    for c in started:
        c.wait_send()


def weight_kernel(sums, enc, att_in, gq_in, gk_in, gv_in, att_out, gq_out, gk_out, gv_out, gw_out, gw, out_sem):
    saves = []
    for n, (src, dst) in enumerate(((att_in, att_out), (gq_in, gq_out), (gk_in, gk_out), (gv_in, gv_out))):
        c = pltpu.make_async_copy(src, dst, out_sem.at[n])
        c.start()
        saves.append(c)
    groups = lane_groups(HEAD)
    for j in range(TILES):
        half, place = j // 5, j % 5
        rows = jnp.concatenate([sums[2 * r + half, :, 128 * place : 128 * (place + 1)] for r in range(8)], axis=0)
        block = enc[4 * j : 4 * j + 4].reshape(128, 128)
        for i in range(4):
            gw[j, :, 128 * i : 128 * (i + 1)] = dot(jnp.where(groups == i, rows, jnp.zeros_like(rows)), block).astype(BF16)
        c = pltpu.make_async_copy(gw.at[j], gw_out.at[:, pl.ds(512 * j, 512)], out_sem.at[4 + j])
        c.start()
        saves.append(c)
    for c in saves:
        c.wait()


def local(q, k, v, w, enc, dec, pos, cot):
    any_ = pl.BlockSpec(memory_space=pl.ANY)
    hbm = pl.BlockSpec(memory_space=pltpu.HBM)
    vmem = pl.BlockSpec(memory_space=pltpu.VMEM)

    def shape(*dims):
        return jax.ShapeDtypeStruct(dims, BF16)

    n_copies = 50
    operands = (q, k, v, w, enc.transpose(0, 2, 1), dec, pos, cot)
    row_shapes = (shape(OWN, WIDTH), shape(LEN, HEAD), shape(LEN, HEAD), shape(LEN, HEAD))
    sums, att, gq, gk, gv, enc_kept = pl.pallas_call(
        core_kernel,
        out_shape=(shape(DP, 16, 640), *row_shapes, shape(40, 32, 128)),
        in_specs=[hbm] * 8,
        out_specs=[vmem] * 6,
        scratch_shapes=[
            pltpu.VMEM((LEN, HEAD), BF16),
            pltpu.VMEM((LEN, HEAD), BF16),
            pltpu.VMEM((LEN, HEAD), BF16),
            pltpu.VMEM((HEAD, WIDTH), BF16),
            pltpu.VMEM((40, 32, 128), BF16),
            pltpu.VMEM((LEN,), jnp.int32),
            pltpu.VMEM((OWN, WIDTH), BF16),
            pltpu.VMEM((PAD, WIDTH), F32),
            pltpu.VMEM((MSG, 128), F32),
            pltpu.VMEM((2, 4, 4, MSG, 128), BF16),
            pltpu.VMEM((16, MSG, 128), F32),
            pltpu.VMEM((SLOTS * PAD, CODE), BF16),
            pltpu.VMEM((SLOTS * PAD, LEN), BF16),
            pltpu.VMEM((SLOTS * PAD, LEN), F32),
            pltpu.VMEM((SLOTS * PAD, HEAD), BF16),
            pltpu.VMEM((HEAD, SLOTS * PAD), BF16),
            pltpu.VMEM((TILES, 128, 512), BF16),
            pltpu.VMEM((HEAD, CODE), BF16),
            pltpu.VMEM((SLOTS, MSG, 128), F32),
            pltpu.VMEM((4, 4, MSG, 128), BF16),
            pltpu.VMEM((4, 4, MSG, 128), BF16),
            pltpu.VMEM((4, 4, MSG, 128), BF16),
            pltpu.VMEM((4, 4, MSG, 128), BF16),
            pltpu.VMEM((4, MSG, 128), BF16),
            pltpu.VMEM((4, MSG, 128), BF16),
            pltpu.VMEM((MSG, 128), F32),
            pltpu.VMEM((DP, 16, 640), BF16),
            pltpu.VMEM((DP, 16, 640), BF16),
            pltpu.VMEM((DP, 16, 640), BF16),
            pltpu.SemaphoreType.DMA((8,)),
            pltpu.SemaphoreType.DMA((n_copies,)),
            pltpu.SemaphoreType.DMA((n_copies,)),
        ],
        compiler_params=pltpu.CompilerParams(
            collective_id=0, has_side_effects=True, vmem_limit_bytes=48 * 2**20
        ),
        name="attention_and_sums",
    )(*[pltpu.with_memory_space_constraint(a, pltpu.HBM) for a in operands])
    return pl.pallas_call(
        weight_kernel,
        out_shape=(*row_shapes, shape(HEAD, WIDTH)),
        in_specs=[vmem] * 6,
        out_specs=[any_] * 5,
        scratch_shapes=[
            pltpu.VMEM((TILES, HEAD, 512), BF16),
            pltpu.SemaphoreType.DMA((4 + TILES,)),
        ],
        compiler_params=pltpu.CompilerParams(vmem_limit_bytes=16 * 2**20),
        name="weight_gradient",
    )(sums, enc_kept, att, gq, gk, gv)


def solution(mesh):
    return jax.shard_map(
        local,
        mesh=mesh,
        in_specs=(
            P("dp", "tensor"), P("dp", "tensor"), P("dp", "tensor"), P("tensor", None),
            P(), P(), P("dp"), P(("dp", "tensor"), None),
        ),
        out_specs=(
            P(("dp", "tensor"), None), P("dp", "tensor"), P("dp", "tensor"), P("dp", "tensor"), P("tensor", None),
        ),
        check_vma=False,
    )
```

time: 351 us -> 46.7 us (0.13)
  waiting for transfers between devices: 271 us -> 0 us
  Pallas kernels: 0 us -> 45.9 us
  blocking collectives: 39.4 us -> 0 us
  between operations: 14.9 us -> 0.64 us
  matrix products: 13.2 us -> 0 us
  local copies, waits for them, and re-layouts: 11.3 us -> 0 us
    unnamed x3 -> x0, waiting for transfers between devices: 153 us -> none
    psum x1 -> x0, waiting for transfers between devices: 118 us -> none  [local(): grad_weight = lax.psum(weight_acc.astype(jnp.bfloat16), 'dp')]
    pallas_call x0 -> x2, Pallas kernels: none -> 45.9 us  [the longest x1 44.6 us: local(): pl.pallas_call(core_kernel, out_shape=(shape(DP, 16, 640), *row_shapes, s...]
    all_gather x1 -> x0, blocking collectives: 39.4 us -> none  [local(): lax.all_gather(grad_code, 'tensor', axis=0, tiled=True).astype(jnp.float32)]
    dot_general x14 -> x0, matrix products: 13.2 us -> none  [the longest x1 3.22 us: encode(): jnp.einsum('rbi,bio->rbo', shaped, encoder.astype(jnp.float32), precision...]
    unnamed x22 -> x0, local copies, waits for them, and re-layouts: 7.09 us -> none
  transfers between devices with their start and end apart: 2 -> 0, of which waited for: 2 -> 0; matrix products, arithmetic and copies ran while one was open for 4% -> 0% of each run, Pallas kernels for 0% -> 0%
where the time goes in v1:
time: 46.7 us; the launch traced here: 46.6 us
  Pallas kernels  45.9 us (98%)
  between operations  0.64 us (1%)
    pallas_call x1, Pallas kernels, local(): pl.pallas_call(core_kernel, out_shape=(shape(DP, 16, 640), *row_shapes, s...  44.6 us
    pallas_call x1, Pallas kernels, local(): pl.pallas_call(weight_kernel, out_shape=(*row_shapes, shape(HEAD, WIDTH))...  1.36 us

profile of v1, /device:TPU:1, one launch (start us, length us, event | category | flops | bytes accessed | tf_op | source)
XLA Modules:
  0.0 46.6 jit_solution(12359993456095058168)
XLA Ops:
  0.6 44.6 %attention_and_sums.1 = (bf16[16,16,640]{2,1,0:T(8,128)(2,1)S(1)}, bf16[5,5120]{1,0:T(8,128)(2,1)S(1)}, bf16[160,128]{1,0:T(8,128)(2,1)S(1)}, bf16[160,128]{1,0:...) custom-call(bf16[160,128]{1,0:T(8,128)(2,1)} %q_hbm.1, bf16[160,128]{1,0:T(8,128)(2,1)} %k_hbm.1, ...), custom_call_target="tpu_custom_call" | custom-call | tf_op jit(solution)/shard_map/attention_and_sums/pallas_call | solution.py:268
  45.2 1.4 %weight_gradient.1 = (bf16[5,5120]{1,0:T(8,128)(2,1)}, bf16[160,128]{1,0:T(8,128)(2,1)}, bf16[160,128]{1,0:T(8,128)(2,1)}, bf16[160,128]{1,0:T(8,128)(2,1)}, bf16[128,5120]{1,0:T(8,128)(2,1)}) custom-call(bf16[16,16,640]{2,1,0:T(8,128)(2,1)S(1)} %get-tuple-element.11.sums, bf16[40,32,128]{2,1,0:T(8,128)(2,1)S(1)} %get-tuple-element.12.enc, ...), custom_call_target="tpu_custom_call" | custom-call | tf_op jit(solution)/shard_map/weight_gradient/pallas_call | solution.py:312

commit v2 on v1

--- a/solution.py
+++ b/solution.py
@@ -23,6 +23,8 @@
 DP = 16
 NT = (((1,), (1,)), ((), ()))
 TN = (((0,), (0,)), ((), ()))
+NEAR = (0, 1, -1)
+FAR = (0, 3, -3, 6, -6)
 
 
 def dot(a, b, dims=(((1,), (0,)), ((), ()))):
@@ -35,9 +37,9 @@
 
 def core_kernel(
     q_hbm, k_hbm, v_hbm, w_hbm, enc_hbm, dec_hbm, pos_hbm, cot_hbm,
-    sum_out, att_out, gq_out, gk_out, gv_out, enc,
+    sum_a_out, sum_b_out, att_out, gq_out, gk_out, gv_out, enc,
     q, k, v, w, dec, pos, cot, cot8, gst, gbuf, ust, gpad, perm, attn, ctx, ctx_t, spread, wenc,
-    pst, psnd, psib, pone, prec1, ptwo, prec2, code, mpart, mrecv, mfull,
+    pst, psnd, psib, pone, prec1, prec15, ptwo, prec2, code, part_a, part_b, recv_a, recv_b, full_a, full_b,
     in_sem, send_sem, recv_sem,
 ):
     dp = lax.axis_index("dp")
@@ -50,8 +52,13 @@
 
     sibling = {"tensor": t + sign}
 
+    def plane_at(d):
+        return lax.rem(dp // 4 + d // 4, 4) * 4 + lax.rem(dp + d, 4)
+
     def plane(d):
-        return {"dp": lax.rem(dp + d, DP)}
+        return {"dp": plane_at(d)}
+
+    offsets = sorted(range(1, DP), key=lambda d: -min(d // 4, 4 - d // 4) - min(d % 4, 4 - d % 4))
 
     loads = []
     for n, (src, dst) in enumerate(
@@ -63,7 +70,7 @@
     cot_in, dec_in, q_in, k_in, v_in, pos_in, enc_in, w_in = loads
 
     barrier = pltpu.get_barrier_semaphore()
-    partners = [sibling] + [chip(dz) for dz in (8, 4, -4, 2, -2, 1, -1)] + [plane(d) for d in range(1, DP)]
+    partners = [sibling] + [chip(dz) for dz in (6, -6, 3, -3, 2, -2, 1, -1)] + [plane(d) for d in offsets]
     for device in partners:
         pl.semaphore_signal(barrier, inc=1, device_id=device, device_id_type=MESH)
 
@@ -94,22 +101,17 @@
         for i in range(4):
             tile = tile + jnp.where(groups8 == i, full[PAD * i : PAD * (i + 1)], 0.0)
         gst[OWN * j : OWN * j + PAD, :] = tile
-    gbuf[0, 0, 0] = gst[...].astype(BF16)
-
-    pl.semaphore_wait(barrier, len(partners))
-
-    steps = (0, 1, 2 * sign, -1)
-    g_far = [None] + [send(gbuf.at[0, 0, 0], gbuf.at[0, 0, 4 - n], chip(4 * n)) for n in (2, 1, 3)]
-    g_near = [None] + [send(gbuf.at[0, 0, 0], gbuf.at[0, p, 0], chip(-steps[p])) for p in (1, 2, 3)]
+    gbuf[0, 0] = gst[...].astype(BF16)
 
     row = lax.broadcasted_iota(jnp.int32, (SLOTS * PAD, LEN), 0)
     col = lax.broadcasted_iota(jnp.int32, (SLOTS * PAD, LEN), 1)
     slot = row // PAD
     other = slot // 16
-    near = (slot // 4) % 4
-    far = slot % 4
-    step = jnp.where(near == 1, 1, jnp.where(near == 2, 2 * sign * (1 - 2 * other), jnp.where(near == 3, -1, 0)))
-    at_chip = (t // 2 + step + 4 * far + 16) % 16
+    place = slot % 16
+    step = jnp.full_like(row, 8)
+    for n in range(15):
+        step = jnp.where(place == n, NEAR[n // 5] + FAR[n % 5], step)
+    at_chip = (t // 2 + step + 16) % 16
     token = OWN * (2 * at_chip + (core + other) % 2) + row % PAD
     valid = row % PAD < OWN
     perm[...] = jnp.where(valid & (token == col), 1.0, 0.0).astype(BF16)
@@ -143,59 +145,76 @@
     for j in range(TILES):
         part = dot(w[:, 512 * j : 512 * (j + 1)], spread[j], NT).astype(BF16)
         wenc[:, 128 * j : 128 * (j + 1)] = part
-        pst[:, OWN * j : OWN * j + PAD, :] = dot(ctx[...], part).reshape(SLOTS, PAD, 128)
+    for j in range(TILES):
+        part = dot(ctx[...], wenc[:, 128 * j : 128 * (j + 1)])
+        pst[:, OWN * j : OWN * j + PAD, :] = part.reshape(SLOTS, PAD, 128)
     pst[:, MSG - 8 : MSG, :] = jnp.zeros((SLOTS, 8, 128), F32)
-    psnd[...] = pst[16:32].reshape(4, 4, MSG, 128).astype(BF16)
+    psnd[...] = pst[16:32].astype(BF16)
+    pl.semaphore_wait(barrier, len(partners))
+
+    own = gbuf.at[0, 0]
+    g_far = {}
+    for n in (3, 4, 1, 2):
+        back = n + 1 if n % 2 else n - 1
+        g_far[n] = send(own, gbuf.at[0, back], chip(FAR[n]))
+    g_near = {p: send(own, gbuf.at[0, 5 * p], chip(-NEAR[p])) for p in (1, 2)}
     p_sib = send(psnd, psib, sibling)
 
-    for c in g_far[1:]:
-        c.wait_recv()
-    g_pack = [None] + [send(gbuf.at[0, 0, pl.ds(1, 3)], gbuf.at[0, p, pl.ds(1, 3)], chip(-steps[p])) for p in (1, 2, 3)]
-    g_over = [send(gbuf.at[0, 0], gbuf.at[1, 0], sibling)]
-
     p_sib.wait_recv()
-    for p in range(4):
-        pst[4 * p : 4 * p + 4] = pst[4 * p : 4 * p + 4] + psib[p].astype(F32)
-        if p:
-            pone[p] = pst[4 * p : 4 * p + 4].astype(BF16)
-    p_near = [None] + [send(pone.at[p], prec1.at[p], chip(steps[p])) for p in (1, 2, 3)]
+    for n in range(16):
+        pst[n] = pst[n] + psib[n].astype(F32)
+        if n >= 5:
+            pone[n] = pst[n].astype(BF16)
+    p_near = [send(pone.at[pl.ds(5 * p, 5)], prec1.at[p], chip(NEAR[p])) for p in (1, 2)]
+    p_near.append(send(pone.at[15], prec15, chip(2 * sign)))
 
     def unpack(other_core):
-        for p in range(4):
-            ust[4 * p : 4 * p + 4] = gbuf[other_core, p].astype(F32)
+        ust[...] = gbuf[other_core].astype(F32)
         keep = lax.broadcasted_iota(jnp.int32, (16, PAD, 128), 1) < OWN
         for j in range(TILES):
             block = jnp.where(keep, ust[:, OWN * j : OWN * j + PAD, :], 0.0)
             gpad[128 * other_core : 128 * (other_core + 1), 128 * j : 128 * (j + 1)] = block.reshape(128, 128).astype(BF16)
 
-    for p in (1, 3, 2):
+    g_pack = {}
+    for part in (1, 3):
+        g_far[part].wait_recv()
+        g_far[part + 1].wait_recv()
+        for p in (1, 2):
+            block = pl.ds(5 * p + part, 2)
+            g_pack[p, part] = send(gbuf.at[0, pl.ds(part, 2)], gbuf.at[0, block], chip(-NEAR[p]))
+    g_last = send(gbuf.at[0, 3 + core], gbuf.at[0, 15], chip(-2 * sign))
+    g_over = [send(gbuf.at[0, pl.ds(0, 5)], gbuf.at[1, pl.ds(0, 5)], sibling)]
+    for c in p_near:
+        c.wait_recv()
+    for n in range(5):
+        total = pst[n] + prec1[1, n].astype(F32) + prec1[2, n].astype(F32)
+        if n >= 3:
+            total = total + jnp.where(core == n - 3, prec15[...].astype(F32), 0.0)
+        if n:
+            ptwo[n] = total.astype(BF16)
+        else:
+            code[0:MSG] = total
+    p_far = [send(ptwo.at[n], prec2.at[n], chip(FAR[n])) for n in (3, 4, 1, 2)]
+    for p in (1, 2):
         g_near[p].wait_recv()
-        g_pack[p].wait_recv()
-        g_over.append(send(gbuf.at[0, p], gbuf.at[1, p], sibling))
+        g_pack[p, 1].wait_recv()
+        g_over.append(send(gbuf.at[0, pl.ds(5 * p, 3)], gbuf.at[1, pl.ds(5 * p, 3)], sibling))
+    for p in (1, 2):
+        g_pack[p, 3].wait_recv()
+        g_over.append(send(gbuf.at[0, pl.ds(5 * p + 3, 2)], gbuf.at[1, pl.ds(5 * p + 3, 2)], sibling))
+    g_last.wait_recv()
+    g_over.append(send(gbuf.at[0, 15], gbuf.at[1, 15], sibling))
     unpack(0)
     for c in g_over:
         c.wait_recv()
     unpack(1)
 
-    for half in range(2):
-        part = dot(ctx_t[...], gpad[:, 640 * half : 640 * (half + 1)]).astype(BF16)
-        for r in range(8):
-            mpart[2 * r + half] = part[16 * r : 16 * (r + 1)]
     m_parts = []
-    for d in range(1, DP):
-        m_parts.append(send(mpart.at[lax.rem(dp + d, DP)], mrecv.at[d], plane(d)))
-
-    for c in p_near[1:]:
-        c.wait_recv()
-    for n in range(4):
-        total = pst[n]
-        for p in (1, 2, 3):
-            total = total + prec1[p, n].astype(F32)
-        if n:
-            ptwo[n] = total.astype(BF16)
-        else:
-            code[0:MSG] = total
-    p_far = [None] + [send(ptwo.at[n], prec2.at[n], chip(4 * n)) for n in (2, 1, 3)]
+    for start, width, part, recv in ((0, 768, part_a, recv_a), (768, 512, part_b, recv_b)):
+        grad = dot(ctx_t[...], gpad[:, start : start + width]).astype(BF16)
+        for r in range(DP):
+            part[r] = grad[16 * (r // 2) : 16 * (r // 2 + 1), width // 2 * (r % 2) : width // 2 * (r % 2 + 1)]
+        m_parts.append([send(part.at[plane_at(d)], recv.at[d], plane(d)) for d in offsets])
 
     gc = dot(gpad[...], wenc[...], NT).astype(BF16)
     probs = attn[...]
@@ -206,18 +225,19 @@
     gq_out[...] = dot(perm[...], dot(g_score, k[...]).astype(BF16), TN).astype(BF16)
     gk_out[...] = dot(g_score, qp, TN).astype(BF16)
 
-    for c in m_parts:
-        c.wait_recv()
-    total = mpart[dp].astype(F32)
-    for d in range(1, DP):
-        total = total + mrecv[d].astype(F32)
-    mfull[dp] = total.astype(BF16)
-    m_sums = [send(mfull.at[dp], mfull.at[dp], plane(d)) for d in range(1, DP)]
-
-    for c in p_far[1:]:
+    m_sums = []
+    for copies, part, recv, full in ((m_parts[0], part_a, recv_a, full_a), (m_parts[1], part_b, recv_b, full_b)):
+        total = part[dp].astype(F32)
+        for d, c in zip(offsets, copies):
+            c.wait_recv()
+            total = total + recv[d].astype(F32)
+        full[dp] = total.astype(BF16)
+        m_sums += [send(full.at[dp], full.at[dp], plane(d)) for d in offsets]
+
+    for c in p_far:
         c.wait_recv()
     total = code[0:MSG]
-    for n in (1, 2, 3):
+    for n in (1, 2, 3, 4):
         total = total + prec2[n].astype(F32)
     code[0:MSG] = total
     for j in range(TILES):
@@ -229,12 +249,13 @@
 
     for c in m_sums:
         c.wait_recv()
-    sum_out[...] = mfull[...]
+    sum_a_out[...] = full_a[...]
+    sum_b_out[...] = full_b[...]
     for c in started:
         c.wait_send()
 
 
-def weight_kernel(sums, enc, att_in, gq_in, gk_in, gv_in, att_out, gq_out, gk_out, gv_out, gw_out, gw, out_sem):
+def weight_kernel(sum_a, sum_b, enc, att_in, gq_in, gk_in, gv_in, att_out, gq_out, gk_out, gv_out, gw_out, gw, out_sem):
     saves = []
     for n, (src, dst) in enumerate(((att_in, att_out), (gq_in, gq_out), (gk_in, gk_out), (gv_in, gv_out))):
         c = pltpu.make_async_copy(src, dst, out_sem.at[n])
@@ -242,7 +263,8 @@
         saves.append(c)
     groups = lane_groups(HEAD)
     for j in range(TILES):
-        half, place = j // 5, j % 5
+        sums, wide, at = (sum_a, 3, j) if j < 6 else (sum_b, 2, j - 6)
+        half, place = at // wide, at % wide
         rows = jnp.concatenate([sums[2 * r + half, :, 128 * place : 128 * (place + 1)] for r in range(8)], axis=0)
         block = enc[4 * j : 4 * j + 4].reshape(128, 128)
         for i in range(4):
@@ -262,14 +284,14 @@
     def shape(*dims):
         return jax.ShapeDtypeStruct(dims, BF16)
 
-    n_copies = 50
+    n_copies = 85
     operands = (q, k, v, w, enc.transpose(0, 2, 1), dec, pos, cot)
     row_shapes = (shape(OWN, WIDTH), shape(LEN, HEAD), shape(LEN, HEAD), shape(LEN, HEAD))
-    sums, att, gq, gk, gv, enc_kept = pl.pallas_call(
+    sum_a, sum_b, att, gq, gk, gv, enc_kept = pl.pallas_call(
         core_kernel,
-        out_shape=(shape(DP, 16, 640), *row_shapes, shape(40, 32, 128)),
+        out_shape=(shape(DP, 16, 384), shape(DP, 16, 256), *row_shapes, shape(40, 32, 128)),
         in_specs=[hbm] * 8,
-        out_specs=[vmem] * 6,
+        out_specs=[vmem] * 7,
         scratch_shapes=[
             pltpu.VMEM((LEN, HEAD), BF16),
             pltpu.VMEM((LEN, HEAD), BF16),
@@ -280,7 +302,7 @@
             pltpu.VMEM((OWN, WIDTH), BF16),
             pltpu.VMEM((PAD, WIDTH), F32),
             pltpu.VMEM((MSG, 128), F32),
-            pltpu.VMEM((2, 4, 4, MSG, 128), BF16),
+            pltpu.VMEM((2, 16, MSG, 128), BF16),
             pltpu.VMEM((16, MSG, 128), F32),
             pltpu.VMEM((SLOTS * PAD, CODE), BF16),
             pltpu.VMEM((SLOTS * PAD, LEN), BF16),
@@ -290,16 +312,20 @@
             pltpu.VMEM((TILES, 128, 512), BF16),
             pltpu.VMEM((HEAD, CODE), BF16),
             pltpu.VMEM((SLOTS, MSG, 128), F32),
-            pltpu.VMEM((4, 4, MSG, 128), BF16),
-            pltpu.VMEM((4, 4, MSG, 128), BF16),
-            pltpu.VMEM((4, 4, MSG, 128), BF16),
-            pltpu.VMEM((4, 4, MSG, 128), BF16),
-            pltpu.VMEM((4, MSG, 128), BF16),
-            pltpu.VMEM((4, MSG, 128), BF16),
+            pltpu.VMEM((16, MSG, 128), BF16),
+            pltpu.VMEM((16, MSG, 128), BF16),
+            pltpu.VMEM((16, MSG, 128), BF16),
+            pltpu.VMEM((3, 5, MSG, 128), BF16),
+            pltpu.VMEM((MSG, 128), BF16),
+            pltpu.VMEM((5, MSG, 128), BF16),
+            pltpu.VMEM((5, MSG, 128), BF16),
             pltpu.VMEM((MSG, 128), F32),
-            pltpu.VMEM((DP, 16, 640), BF16),
-            pltpu.VMEM((DP, 16, 640), BF16),
-            pltpu.VMEM((DP, 16, 640), BF16),
+            pltpu.VMEM((DP, 16, 384), BF16),
+            pltpu.VMEM((DP, 16, 256), BF16),
+            pltpu.VMEM((DP, 16, 384), BF16),
+            pltpu.VMEM((DP, 16, 256), BF16),
+            pltpu.VMEM((DP, 16, 384), BF16),
+            pltpu.VMEM((DP, 16, 256), BF16),
             pltpu.SemaphoreType.DMA((8,)),
             pltpu.SemaphoreType.DMA((n_copies,)),
             pltpu.SemaphoreType.DMA((n_copies,)),
@@ -312,7 +338,7 @@
     return pl.pallas_call(
         weight_kernel,
         out_shape=(*row_shapes, shape(HEAD, WIDTH)),
-        in_specs=[vmem] * 6,
+        in_specs=[vmem] * 7,
         out_specs=[any_] * 5,
         scratch_shapes=[
             pltpu.VMEM((TILES, HEAD, 512), BF16),
@@ -320,7 +346,7 @@
         ],
         compiler_params=pltpu.CompilerParams(vmem_limit_bytes=16 * 2**20),
         name="weight_gradient",
-    )(sums, enc_kept, att, gq, gk, gv)
+    )(sum_a, sum_b, enc_kept, att, gq, gk, gv)
 
 
 def solution(mesh):

time: 46.7 us -> 43.4 us (0.929)
  Pallas kernels: 45.9 us -> 42.6 us
    pallas_call x1, Pallas kernels: 44.6 us -> 41.2 us  [local(): pl.pallas_call(core_kernel, out_shape=(shape(DP, 16, 384), shape(DP, 16,...]
where the time goes in v2:
time: 43.4 us; the launch traced here: 43.2 us
  Pallas kernels  42.6 us (98%)
  between operations  0.64 us (1%)
    pallas_call x1, Pallas kernels, local(): pl.pallas_call(core_kernel, out_shape=(shape(DP, 16, 384), shape(DP, 16,...  41.2 us
    pallas_call x1, Pallas kernels, local(): pl.pallas_call(weight_kernel, out_shape=(*row_shapes, shape(HEAD, WIDTH))...  1.36 us

profile of v2, /device:TPU:1, one launch (start us, length us, event | category | flops | bytes accessed | tf_op | source)
XLA Modules:
  0.0 43.2 jit_solution(18230654313462946384)
XLA Ops:
  0.6 41.2 %attention_and_sums.1 = (bf16[16,16,384]{2,1,0:T(8,128)(2,1)S(1)}, bf16[16,16,256]{2,1,0:T(8,128)(2,1)S(1)}, bf16[5,5120]{1,0:T(8,128)(2,1)S(1)}, bf16[160,128]{...) custom-call(bf16[160,128]{1,0:T(8,128)(2,1)} %q_hbm.1, ...), custom_call_target="tpu_custom_call" | custom-call | tf_op jit(solution)/shard_map/attention_and_sums/pallas_call | solution.py:290
  41.9 1.4 %weight_gradient.1 = (bf16[5,5120]{1,0:T(8,128)(2,1)}, bf16[160,128]{1,0:T(8,128)(2,1)}, bf16[160,128]{1,0:T(8,128)(2,1)}, bf16[160,128]{1,0:T(8,128)(2,1)}, bf16[128,5120]{1,0:T(8,128)(2,1)}) custom-call(bf16[16,16,384]{2,1,0:T(8,128)(2,1)S(1)} %get-tuple-element.12.sum_a, bf16[16,16,256]{2,1,0:T(8,128)(2,1)S(1)} %get-tuple-element.13.sum_b, ...), custom_call_target="tpu_custom_call" | custom-call | tf_op jit(solution)/shard_map/weight_gradient/pallas_call | solution.py:338

commit v3 on v2

--- a/solution.py
+++ b/solution.py
@@ -25,6 +25,8 @@
 TN = (((0,), (0,)), ((), ()))
 NEAR = (0, 1, -1)
 FAR = (0, 3, -3, 6, -6)
+PARTS = ((0, 4), (4, 6))
+LAST = len(PARTS) - 1
 
 
 def dot(a, b, dims=(((1,), (0,)), ((), ()))):
@@ -35,13 +37,22 @@
     return lax.broadcasted_iota(jnp.int32, (rows, 128), 1) // 32
 
 
+def expand(sums, wide, at, block):
+    half, place = at // wide, at % wide
+    rows = jnp.concatenate([sums[2 * r + half, :, 128 * place : 128 * (place + 1)] for r in range(8)], axis=0)
+    groups = lane_groups(HEAD)
+    return [dot(jnp.where(groups == i, rows, jnp.zeros_like(rows)), block).astype(BF16) for i in range(4)]
+
+
 def core_kernel(
     q_hbm, k_hbm, v_hbm, w_hbm, enc_hbm, dec_hbm, pos_hbm, cot_hbm,
-    sum_a_out, sum_b_out, att_out, gq_out, gk_out, gv_out, enc,
+    gw_out, last_out, att_out, gq_out, gk_out, gv_out, enc,
     q, k, v, w, dec, pos, cot, cot8, gst, gbuf, ust, gpad, perm, attn, ctx, ctx_t, spread, wenc,
-    pst, psnd, psib, pone, prec1, prec15, ptwo, prec2, code, part_a, part_b, recv_a, recv_b, full_a, full_b,
-    in_sem, send_sem, recv_sem,
+    pst, psnd, psib, pone, prec1, prec15, ptwo, prec2, code, *rest,
 ):
+    n_parts = len(PARTS)
+    parts, recvs, fulls = rest[:n_parts], rest[n_parts : 2 * n_parts], rest[2 * n_parts : 3 * n_parts]
+    in_sem, send_sem, recv_sem = rest[3 * n_parts :]
     dp = lax.axis_index("dp")
     t = lax.axis_index("tensor")
     core = lax.rem(t, 2)
@@ -52,6 +63,10 @@
 
     sibling = {"tensor": t + sign}
 
+    def across(dz):
+        return {"tensor": lax.rem(t + sign + 2 * dz + SLOTS, SLOTS)}
+
+
     def plane_at(d):
         return lax.rem(dp // 4 + d // 4, 4) * 4 + lax.rem(dp + d, 4)
 
@@ -59,6 +74,12 @@
         return {"dp": plane_at(d)}
 
     offsets = sorted(range(1, DP), key=lambda d: -min(d // 4, 4 - d // 4) - min(d % 4, 4 - d % 4))
+
+    barrier = pltpu.get_barrier_semaphore()
+    partners = [sibling] + [chip(dz) for dz in (6, -6, 3, -3, 2, -2, 1, -1)]
+    partners += [across(dz) for dz in (-2 * sign, 1, -1)] + [plane(d) for d in offsets]
+    for device in partners:
+        pl.semaphore_signal(barrier, inc=1, device_id=device, device_id_type=MESH)
 
     loads = []
     for n, (src, dst) in enumerate(
@@ -68,11 +89,6 @@
         c.start()
         loads.append(c)
     cot_in, dec_in, q_in, k_in, v_in, pos_in, enc_in, w_in = loads
-
-    barrier = pltpu.get_barrier_semaphore()
-    partners = [sibling] + [chip(dz) for dz in (6, -6, 3, -3, 2, -2, 1, -1)] + [plane(d) for d in offsets]
-    for device in partners:
-        pl.semaphore_signal(barrier, inc=1, device_id=device, device_id_type=MESH)
 
     count = [0]
     started = []
@@ -182,8 +198,31 @@
         for p in (1, 2):
             block = pl.ds(5 * p + part, 2)
             g_pack[p, part] = send(gbuf.at[0, pl.ds(part, 2)], gbuf.at[0, block], chip(-NEAR[p]))
-    g_last = send(gbuf.at[0, 3 + core], gbuf.at[0, 15], chip(-2 * sign))
+    g_last = [send(gbuf.at[0, 3 + core], gbuf.at[0, 15], chip(-2 * sign))]
+    g_last.append(send(gbuf.at[0, 3 + core], gbuf.at[1, 15], across(-2 * sign)))
+    for p in (1, 2):
+        g_last.append(send(gbuf.at[0, pl.ds(3, 2)], gbuf.at[1, pl.ds(5 * p + 3, 2)], across(-NEAR[p])))
     g_over = [send(gbuf.at[0, pl.ds(0, 5)], gbuf.at[1, pl.ds(0, 5)], sibling)]
+    for p in (1, 2):
+        g_near[p].wait_recv()
+        g_pack[p, 1].wait_recv()
+        g_over.append(send(gbuf.at[0, pl.ds(5 * p, 3)], gbuf.at[1, pl.ds(5 * p, 3)], sibling))
+    for p in (1, 2):
+        g_pack[p, 3].wait_recv()
+    g_last[0].wait_recv()
+    unpack(0)
+    for c in g_over + g_last[1:]:
+        c.wait_recv()
+    unpack(1)
+
+    m_parts = []
+    for (first, wide), part, recv in zip(PARTS, parts, recvs):
+        width = 128 * wide
+        grad = dot(ctx_t[...], gpad[:, 128 * first : 128 * first + width]).astype(BF16)
+        for r in range(DP):
+            part[r] = grad[16 * (r // 2) : 16 * (r // 2 + 1), width // 2 * (r % 2) : width // 2 * (r % 2 + 1)]
+        m_parts.append([send(part.at[plane_at(d)], recv.at[d], plane(d)) for d in offsets])
+
     for c in p_near:
         c.wait_recv()
     for n in range(5):
@@ -195,27 +234,6 @@
         else:
             code[0:MSG] = total
     p_far = [send(ptwo.at[n], prec2.at[n], chip(FAR[n])) for n in (3, 4, 1, 2)]
-    for p in (1, 2):
-        g_near[p].wait_recv()
-        g_pack[p, 1].wait_recv()
-        g_over.append(send(gbuf.at[0, pl.ds(5 * p, 3)], gbuf.at[1, pl.ds(5 * p, 3)], sibling))
-    for p in (1, 2):
-        g_pack[p, 3].wait_recv()
-        g_over.append(send(gbuf.at[0, pl.ds(5 * p + 3, 2)], gbuf.at[1, pl.ds(5 * p + 3, 2)], sibling))
-    g_last.wait_recv()
-    g_over.append(send(gbuf.at[0, 15], gbuf.at[1, 15], sibling))
-    unpack(0)
-    for c in g_over:
-        c.wait_recv()
-    unpack(1)
-
-    m_parts = []
-    for start, width, part, recv in ((0, 768, part_a, recv_a), (768, 512, part_b, recv_b)):
-        grad = dot(ctx_t[...], gpad[:, start : start + width]).astype(BF16)
-        for r in range(DP):
-            part[r] = grad[16 * (r // 2) : 16 * (r // 2 + 1), width // 2 * (r % 2) : width // 2 * (r % 2 + 1)]
-        m_parts.append([send(part.at[plane_at(d)], recv.at[d], plane(d)) for d in offsets])
-
     gc = dot(gpad[...], wenc[...], NT).astype(BF16)
     probs = attn[...]
     gv_out[...] = dot(probs.astype(BF16), gc, TN).astype(BF16)
@@ -226,13 +244,13 @@
     gk_out[...] = dot(g_score, qp, TN).astype(BF16)
 
     m_sums = []
-    for copies, part, recv, full in ((m_parts[0], part_a, recv_a, full_a), (m_parts[1], part_b, recv_b, full_b)):
+    for copies, part, recv, full in zip(m_parts, parts, recvs, fulls):
         total = part[dp].astype(F32)
         for d, c in zip(offsets, copies):
             c.wait_recv()
             total = total + recv[d].astype(F32)
         full[dp] = total.astype(BF16)
-        m_sums += [send(full.at[dp], full.at[dp], plane(d)) for d in offsets]
+        m_sums.append([send(full.at[dp], full.at[dp], plane(d)) for d in offsets])
 
     for c in p_far:
         c.wait_recv()
@@ -247,29 +265,33 @@
         for i in range(4):
             att_out[:, 512 * j + 128 * i : 512 * j + 128 * (i + 1)] = full[PAD * i : PAD * i + OWN].astype(BF16)
 
-    for c in m_sums:
-        c.wait_recv()
-    sum_a_out[...] = full_a[...]
-    sum_b_out[...] = full_b[...]
     for c in started:
         c.wait_send()
-
-
-def weight_kernel(sum_a, sum_b, enc, att_in, gq_in, gk_in, gv_in, att_out, gq_out, gk_out, gv_out, gw_out, gw, out_sem):
+    for (first, wide), full, copies in zip(PARTS, fulls, m_sums):
+        for c in copies:
+            c.wait_recv()
+        if first == PARTS[LAST][0]:
+            last_out[...] = full[...]
+            break
+        for j in range(first, first + wide):
+            block = enc[4 * j : 4 * j + 4].reshape(128, 128)
+            for i, tile in enumerate(expand(full, wide // 2, j - first, block)):
+                gw_out[:, 512 * j + 128 * i : 512 * j + 128 * (i + 1)] = tile
+
+
+def weight_kernel(gw_head, last, enc, att_in, gq_in, gk_in, gv_in, att_out, gq_out, gk_out, gv_out, gw_out, gw, out_sem):
     saves = []
-    for n, (src, dst) in enumerate(((att_in, att_out), (gq_in, gq_out), (gk_in, gk_out), (gv_in, gv_out))):
+    first, wide = PARTS[LAST]
+    head = gw_out.at[:, pl.ds(0, 512 * first)]
+    for n, (src, dst) in enumerate(((gw_head, head), (att_in, att_out), (gq_in, gq_out), (gk_in, gk_out), (gv_in, gv_out))):
         c = pltpu.make_async_copy(src, dst, out_sem.at[n])
         c.start()
         saves.append(c)
-    groups = lane_groups(HEAD)
-    for j in range(TILES):
-        sums, wide, at = (sum_a, 3, j) if j < 6 else (sum_b, 2, j - 6)
-        half, place = at // wide, at % wide
-        rows = jnp.concatenate([sums[2 * r + half, :, 128 * place : 128 * (place + 1)] for r in range(8)], axis=0)
-        block = enc[4 * j : 4 * j + 4].reshape(128, 128)
-        for i in range(4):
-            gw[j, :, 128 * i : 128 * (i + 1)] = dot(jnp.where(groups == i, rows, jnp.zeros_like(rows)), block).astype(BF16)
-        c = pltpu.make_async_copy(gw.at[j], gw_out.at[:, pl.ds(512 * j, 512)], out_sem.at[4 + j])
+    for n in range(wide):
+        block = enc[4 * (first + n) : 4 * (first + n) + 4].reshape(128, 128)
+        for i, tile in enumerate(expand(last, wide // 2, n, block)):
+            gw[n, :, 128 * i : 128 * (i + 1)] = tile
+        c = pltpu.make_async_copy(gw.at[n], gw_out.at[:, pl.ds(512 * (first + n), 512)], out_sem.at[5 + n])
         c.start()
         saves.append(c)
     for c in saves:
@@ -284,12 +306,13 @@
     def shape(*dims):
         return jax.ShapeDtypeStruct(dims, BF16)
 
-    n_copies = 85
+    n_copies = 25 + 2 * (DP - 1) * len(PARTS)
+    shares = [(DP, 16, 64 * wide) for _, wide in PARTS]
     operands = (q, k, v, w, enc.transpose(0, 2, 1), dec, pos, cot)
     row_shapes = (shape(OWN, WIDTH), shape(LEN, HEAD), shape(LEN, HEAD), shape(LEN, HEAD))
-    sum_a, sum_b, att, gq, gk, gv, enc_kept = pl.pallas_call(
+    gw_head, last, att, gq, gk, gv, enc_kept = pl.pallas_call(
         core_kernel,
-        out_shape=(shape(DP, 16, 384), shape(DP, 16, 256), *row_shapes, shape(40, 32, 128)),
+        out_shape=(shape(HEAD, 512 * PARTS[LAST][0]), shape(*shares[LAST]), *row_shapes, shape(40, 32, 128)),
         in_specs=[hbm] * 8,
         out_specs=[vmem] * 7,
         scratch_shapes=[
@@ -320,12 +343,7 @@
             pltpu.VMEM((5, MSG, 128), BF16),
             pltpu.VMEM((5, MSG, 128), BF16),
             pltpu.VMEM((MSG, 128), F32),
-            pltpu.VMEM((DP, 16, 384), BF16),
-            pltpu.VMEM((DP, 16, 256), BF16),
-            pltpu.VMEM((DP, 16, 384), BF16),
-            pltpu.VMEM((DP, 16, 256), BF16),
-            pltpu.VMEM((DP, 16, 384), BF16),
-            pltpu.VMEM((DP, 16, 256), BF16),
+            *[pltpu.VMEM(share, BF16) for share in 3 * shares],
             pltpu.SemaphoreType.DMA((8,)),
             pltpu.SemaphoreType.DMA((n_copies,)),
             pltpu.SemaphoreType.DMA((n_copies,)),
@@ -341,12 +359,12 @@
         in_specs=[vmem] * 7,
         out_specs=[any_] * 5,
         scratch_shapes=[
-            pltpu.VMEM((TILES, HEAD, 512), BF16),
-            pltpu.SemaphoreType.DMA((4 + TILES,)),
+            pltpu.VMEM((PARTS[LAST][1], HEAD, 512), BF16),
+            pltpu.SemaphoreType.DMA((5 + PARTS[LAST][1],)),
         ],
         compiler_params=pltpu.CompilerParams(vmem_limit_bytes=16 * 2**20),
         name="weight_gradient",
-    )(sum_a, sum_b, enc_kept, att, gq, gk, gv)
+    )(gw_head, last, enc_kept, att, gq, gk, gv)
 
 
 def solution(mesh):

time: 43.4 us -> 42.2 us (0.972)
  Pallas kernels: 42.6 us -> 41.4 us
    pallas_call x1, Pallas kernels: 41.2 us -> 40.2 us  [local(): pl.pallas_call(core_kernel, out_shape=(shape(HEAD, 512 * PARTS[LAST][0]),...]
where the time goes in v3:
time: 42.2 us; the launch traced here: 42 us
  Pallas kernels  41.4 us (98%)
  between operations  0.64 us (2%)
    pallas_call x1, Pallas kernels, local(): pl.pallas_call(core_kernel, out_shape=(shape(HEAD, 512 * PARTS[LAST][0]),...  40.2 us
    pallas_call x1, Pallas kernels, local(): pl.pallas_call(weight_kernel, out_shape=(*row_shapes, shape(HEAD, WIDTH))...  1.22 us

profile of v3, /device:TPU:1, one launch (start us, length us, event | category | flops | bytes accessed | tf_op | source)
XLA Modules:
  0.0 42.0 jit_solution(2767745423997715072)
XLA Ops:
  0.6 40.2 %attention_and_sums.1 = (bf16[128,2048]{1,0:T(8,128)(2,1)S(1)}, bf16[16,16,384]{2,1,0:T(8,128)(2,1)S(1)}, bf16[5,5120]{1,0:T(8,128)(2,1)S(1)}, bf16[160,128]{1,0...) custom-call(bf16[160,128]{1,0:T(8,128)(2,1)} %q_hbm.1, ...), custom_call_target="tpu_custom_call" | custom-call | tf_op jit(solution)/shard_map/attention_and_sums/pallas_call | solution.py:313
  40.8 1.2 %weight_gradient.1 = (bf16[5,5120]{1,0:T(8,128)(2,1)}, bf16[160,128]{1,0:T(8,128)(2,1)}, bf16[160,128]{1,0:T(8,128)(2,1)}, bf16[160,128]{1,0:T(8,128)(2,1)}, bf16[128,5120]{1,0:T(8,128)(2,1)}) custom-call(bf16[128,2048]{1,0:T(8,128)(2,1)S(1)} %get-tuple-element.12.gw_head, bf16[16,16,384]{2,1,0:T(8,128)(2,1)S(1)} %get-tuple-element.13.last, ...), custom_call_target="tpu_custom_call" | custom-call | tf_op jit(solution)/shard_map/weight_gradient/pallas_call | solution.py:356

commit v4 on v3

--- a/solution.py
+++ b/solution.py
@@ -252,6 +252,15 @@
         full[dp] = total.astype(BF16)
         m_sums.append([send(full.at[dp], full.at[dp], plane(d)) for d in offsets])
 
+    for c in started:
+        c.wait_send()
+    for (first, wide), full, copies in zip(PARTS[:LAST], fulls, m_sums):
+        for c in copies:
+            c.wait_recv()
+        for j in range(first, first + wide):
+            block = enc[4 * j : 4 * j + 4].reshape(128, 128)
+            for i, tile in enumerate(expand(full, wide // 2, j - first, block)):
+                gw_out[:, 512 * j + 128 * i : 512 * j + 128 * (i + 1)] = tile
     for c in p_far:
         c.wait_recv()
     total = code[0:MSG]
@@ -264,19 +273,9 @@
         full = dot(rows.astype(BF16), dec[4 * j : 4 * j + 4].reshape(128, 128))
         for i in range(4):
             att_out[:, 512 * j + 128 * i : 512 * j + 128 * (i + 1)] = full[PAD * i : PAD * i + OWN].astype(BF16)
-
-    for c in started:
-        c.wait_send()
-    for (first, wide), full, copies in zip(PARTS, fulls, m_sums):
-        for c in copies:
-            c.wait_recv()
-        if first == PARTS[LAST][0]:
-            last_out[...] = full[...]
-            break
-        for j in range(first, first + wide):
-            block = enc[4 * j : 4 * j + 4].reshape(128, 128)
-            for i, tile in enumerate(expand(full, wide // 2, j - first, block)):
-                gw_out[:, 512 * j + 128 * i : 512 * j + 128 * (i + 1)] = tile
+    for c in m_sums[LAST]:
+        c.wait_recv()
+    last_out[...] = fulls[LAST][...]
 
 
 def weight_kernel(gw_head, last, enc, att_in, gq_in, gk_in, gv_in, att_out, gq_out, gk_out, gv_out, gw_out, gw, out_sem):

time: 42.2 us -> 42.2 us (level)
  no operation moved by 1% of the time
where the time goes in v4:
time: 42.2 us; the launch traced here: 42 us
  Pallas kernels  41.4 us (98%)
  between operations  0.64 us (2%)
    pallas_call x1, Pallas kernels, local(): pl.pallas_call(core_kernel, out_shape=(shape(HEAD, 512 * PARTS[LAST][0]),...  40.2 us
    pallas_call x1, Pallas kernels, local(): pl.pallas_call(weight_kernel, out_shape=(*row_shapes, shape(HEAD, WIDTH))...  1.22 us

profile of v4, /device:TPU:1, one launch (start us, length us, event | category | flops | bytes accessed | tf_op | source)
XLA Modules:
  0.0 42.0 jit_solution(12771695262154867273)
XLA Ops:
  0.6 40.2 %attention_and_sums.1 = (bf16[128,2048]{1,0:T(8,128)(2,1)S(1)}, bf16[16,16,384]{2,1,0:T(8,128)(2,1)S(1)}, bf16[5,5120]{1,0:T(8,128)(2,1)S(1)}, bf16[160,128]{1,0...) custom-call(bf16[160,128]{1,0:T(8,128)(2,1)} %q_hbm.1, ...), custom_call_target="tpu_custom_call" | custom-call | tf_op jit(solution)/shard_map/attention_and_sums/pallas_call | solution.py:312
  40.8 1.2 %weight_gradient.1 = (bf16[5,5120]{1,0:T(8,128)(2,1)}, bf16[160,128]{1,0:T(8,128)(2,1)}, bf16[160,128]{1,0:T(8,128)(2,1)}, bf16[160,128]{1,0:T(8,128)(2,1)}, bf16[128,5120]{1,0:T(8,128)(2,1)}) custom-call(bf16[128,2048]{1,0:T(8,128)(2,1)S(1)} %get-tuple-element.12.gw_head, bf16[16,16,384]{2,1,0:T(8,128)(2,1)S(1)} %get-tuple-element.13.last, ...), custom_call_target="tpu_custom_call" | custom-call | tf_op jit(solution)/shard_map/weight_gradient/pallas_call | solution.py:355
